TPU v7x, 256 devices: a whole 4x4x8 slice. The times are simulated.
256 devices in a mesh: frames: 4 (over y), rows: 64 (over x, z, core).
Axes of the slice: x: 4, y: 4, z: 8, core: 2. Of those that a mesh axis runs over, the one named last changes fastest.
Arguments:
- inputs: bfloat16 [4, 256, 424, 256], P('frames', 'rows'), may hold values from -350 to 350, as said below
- cotangent: bfloat16 [4, 256, 424, 256], P('frames', 'rows'), may hold values from -140 to 140, as said below
- kernel: bfloat16 [3, 3, 3, 256, 256], replicated, may hold values from -0.078125 to 0.078125
- norm_gain: float32 [256], replicated, may hold values from 0.1 to 1.9
- norm_bias: float32 [256], replicated, may hold values from -1 to 1
Outputs:
- input_grad: bfloat16 [4, 256, 424, 256], P('frames', 'rows')
Inputs may be any that keep to these rules, and one draw needn't show every extreme that they name: `inputs`: finite values. `cotangent`: finite values.
All inputs are finite; a program needn't handle non-finite values.
Results may differ from a plain program's by a relative error of at most 0.0055.
Values may be sent and summed in bfloat16 or wider, within the bound.
A program may use at most 64 MiB of HBM per device.

v0:
```python
import jax
import jax.numpy as jnp
from jax import lax
from jax.sharding import Mesh
from jax.sharding import PartitionSpec as P

GROUPS = 32
ROWS = ("rows_0", "rows_1", "rows_2")


EPS = 1e-06


def from_behind(value, axis, by):
    devices = lax.axis_size(axis)
    pairs = [(i, i + by) for i in range(devices) if 0 <= i + by < devices]
    return lax.ppermute(value, axis, pairs)


def padded_2(value, sides, width):
    for axis, dim in sides:
        devices, length = (lax.axis_size(axis), value.shape[dim])
        up = [(i, (i + 1) % devices) for i in range(devices - 1)]
        down = [(j, i) for i, j in up]
        last = lax.slice_in_dim(value, length - width, length, axis=dim)
        first = lax.slice_in_dim(value, 0, width, axis=dim)
        before = lax.ppermute(last, axis, up)
        after = lax.ppermute(first, axis, down)
        value = jnp.concatenate([before, value, after], axis=dim)
    return value


def from_everyone(value, axis):
    copies = jnp.broadcast_to(value, (lax.axis_size(axis), *value.shape))
    return lax.all_to_all(copies, axis, split_axis=0, concat_axis=0, tiled=True)


def of_everyone(value, axis):
    return from_everyone(value, axis).sum(axis=0)


def by_axis(value, axes):
    far, near = axes
    return of_everyone(of_everyone(value, near), far)


def together(arrays, axis):
    vector, at, finished = (jnp.concatenate([a.reshape(-1) for a in arrays]), 0, [])
    running = by_axis(vector, axis)
    for a in arrays:
        finished.append(running[at : at + a.size].reshape(a.shape))
        at += a.size
    return tuple(finished)


def group_sum(values):
    per_chan = jnp.sum(values, axis=(0, 1))
    return jnp.sum(per_chan.reshape(GROUPS, -1), axis=1)


def spread_groups(per_group, channels):
    return jnp.repeat(per_group, channels // GROUPS)


def transpose_conv(rimmed, flipped, strip, width, channels):
    padded = jnp.pad(rimmed, ((0, 0), (0, 0), (1, 1), (0, 0)))
    act_grad = jnp.zeros((strip, width, channels), jnp.float32)
    for row_tap in range(3):
        for col_tap in range(3):
            window = padded[
                :, 2 - row_tap : 2 - row_tap + strip, 2 - col_tap : 2 - col_tap + width, :
            ]
            act_grad = act_grad + jnp.einsum(
                "myxo,mco->yxc",
                window,
                flipped[:, row_tap, col_tap],
                preferred_element_type=jnp.float32,
            )
    return act_grad


def shards(inputs, cotangent, kernel, norm_gain, norm_bias):
    values = inputs[0].astype(jnp.float32)
    strip, width, channels = values.shape
    cells_per = lax.axis_size("frames") * lax.axis_size(ROWS) * strip * width * (channels // GROUPS)
    flipped = kernel[::-1]
    own_slab = cotangent[0]
    later = from_behind(own_slab, "frames", -1)
    latest = from_behind(own_slab, "frames", -2)
    stacked = jnp.stack([own_slab, later, latest])
    rimmed = padded_2(stacked, ((ROWS, 1),), 1)
    act_grad = transpose_conv(rimmed, flipped, strip, width, channels)
    totals, squares = together(
        (group_sum(values), group_sum(values * values)), ("frames", ("rows_0", "rows_1", "rows_2"))
    )
    centre = totals / cells_per
    variance = jnp.maximum(squares / cells_per - centre * centre, 0.0)
    centred = values - spread_groups(centre, channels)
    inv_std = spread_groups(lax.rsqrt(variance + EPS), channels)
    normed = centred * inv_std
    preact = normed * norm_gain + norm_bias
    logistic = jax.nn.sigmoid(preact)
    norm_grad = act_grad * logistic * (1.0 + preact * (1.0 - logistic)) * norm_gain
    grad_total, grad_cross = together(
        (group_sum(norm_grad), group_sum(norm_grad * normed)),
        ("frames", ("rows_0", "rows_1", "rows_2")),
    )
    grad_total = grad_total / cells_per
    grad_cross = grad_cross / cells_per
    input_grad = inv_std * (
        norm_grad
        - spread_groups(grad_total, channels)
        - normed * spread_groups(grad_cross, channels)
    )
    return input_grad.astype(jnp.bfloat16)[None]


def solution(mesh):
    finer = Mesh(
        mesh.devices.reshape(mesh.shape["frames"], 4, 8, 2),
        ("frames", "rows_0", "rows_1", "rows_2"),
    )
    placed = (P("frames", ROWS, None, None), P("frames", ROWS, None, None), P(), P(), P())
    return jax.shard_map(
        shards,
        mesh=finer,
        in_specs=placed,
        out_specs=P("frames", ROWS, None, None),
        check_vma=False,
    )
```

profile of v0, /device:TPU:1, one launch (start us, length us, event | category | flops | bytes accessed | tf_op | source)
XLA Modules:
  0.0 118.4 jit_solution(3972577931352302973)
XLA Ops:
  0.0 1.3 %collective-permute-start.1 = (bf16[4,424,256]{2,1,0:T(8,128)(2,1)}, bf16[4,424,256]{2,1,0:T(8,128)(2,1)}, u32[]{:S(2)}, u32[]{:S(2)}) collective-permute-start(bf16[4,424,256]{2,1,0:T(8,128)(2,1)} %bitcast.150), channel_id=1, source_target_pairs={{128,0},{192,64},{129,1},{193,65},{130,2},{194,66},{131,3},{195,67... | collective-permute-start | bytes 2605064 | tf_op jit(solution)/shard_map/ppermute | solution.py:17
  1.3 1.3 %collective-permute-start = (bf16[4,424,256]{2,1,0:T(8,128)(2,1)}, bf16[4,424,256]{2,1,0:T(8,128)(2,1)}, u32[]{:S(2)}, u32[]{:S(2)}) collective-permute-start(bf16[4,424,256]{2,1,0:T(8,128)(2,1)} %bitcast.151), channel_id=1, source_target_pairs={{64,0},{128,64},{192,128},{65,1},{129,65},{193,129},{66,2},{130,66... | collective-permute-start | bytes 2605064 | tf_op jit(solution)/shard_map/ppermute | solution.py:17
  2.6 2.0 %convert_reduce_fusion = f32[256]{0:T(256)} fusion(bf16[1,4,424,256]{3,2,1,0:T(8,128)(2,1)} %param.5), kind=kLoop, calls=%fused_computation.45 | loop fusion | flops 868096 | bytes 869376 | tf_op jit(solution)/shard_map/reduce_sum | solution.py:57
  4.6 0.9 reshape.35
  5.5 2.2 %fusion.42 = f32[256]{0:T(256)} fusion(bf16[1,4,424,256]{3,2,1,0:T(8,128)(2,1)} %param.5), kind=kLoop, calls=%fused_computation.48 | loop fusion | flops 1302272 | bytes 869376 | tf_op jit(solution)/shard_map/reduce_sum | solution.py:57
  7.6 1.4 %reshape.36 = f32[32,8]{1,0:T(8,128)} reshape(f32[256]{0:T(256)} %fusion.42) | data formatting | bytes 2048 | tf_op jit(solution)/shard_map/reshape | solution.py:58
  9.7 0.8 reduce_sum.111
  11.9 13.2 %all-to-all-start = ((f32[64,1,64]{2,1,0:T(1,128)}), f32[64,1,64]{2,1,0:T(1,128)}, u32[]{:S(2)}, u32[]{:S(2)}) async-start(f32[64,1,64]{2,1,0:T(1,128)} %broadcast_in_dim.30), calls=%async_computation | async-start | bytes 65536 | tf_op jit(solution)/shard_map/all_to_all | solution.py:35
  25.1 2.6 %pad_maximum_fusion = (bf16[3,1,424,256]{3,2,0,1:T(8,128)(2,1)}, bf16[3,1,424,256]{3,2,0,1:T(8,128)(2,1)}) fusion(bf16[1,4,424,256]{3,2,0,1:T(8,128)(2,1)} %bitcast.7, bf16[1,4,424,256]{3,2,0,1:T(8,128)(2,1)} %bitcast.6, bf16[1,4,424,256]{3,2,0,1:T(8,128)(2,1)} %bitcast.152), kind=kLoop, calls=%fused_computation.76 | loop fusion | flops 1302528 | bytes 3907584 | tf_op jit(solution)/shard_map/slice | solution.py:26
  27.7 2.7 %collective-permute-start.3 = (bf16[3,1,424,256]{3,2,0,1:T(8,128)(2,1)}, bf16[3,1,424,256]{3,2,0,1:T(8,128)(2,1)}, u32[]{:S(2)}, u32[]{:S(2)}) collective-permute-start(bf16[3,1,424,256]{3,2,0,1:T(8,128)(2,1)} %get-tuple-element.16), channel_id=1, source_target_pairs={{1,0},{2,1},{3,2},{4,3},{5,4},{6,5},{7,6},{8,7},{9,8},{10,9},{11,1... | collective-permute-start | bytes 1953800 | tf_op jit(solution)/shard_map/ppermute | solution.py:28
  30.4 3.8 %collective-permute-start.2 = (bf16[3,1,424,256]{3,2,0,1:T(8,128)(2,1)}, bf16[3,1,424,256]{3,2,0,1:T(8,128)(2,1)}, u32[]{:S(2)}, u32[]{:S(2)}) collective-permute-start(bf16[3,1,424,256]{3,2,0,1:T(8,128)(2,1)} %get-tuple-element.17), channel_id=1, source_target_pairs={{0,1},{1,2},{2,3},{3,4},{4,5},{5,6},{6,7},{7,8},{8,9},{9,10},{10,1... | collective-permute-start | bytes 1953800 | tf_op jit(solution)/shard_map/ppermute | solution.py:27
  34.2 1.9 %fusion.77 = (bf16[3,1,1,256,256]{4,3,2,1,0:T(8,128)(2,1)}, bf16[3,1,1,256,256]{4,3,2,1,0:T(8,128)(2,1)}, bf16[3,1,1,256,256]{4,3,2,1,0:T(8,128)(2,1)}, bf16[3,1...) fusion(bf16[3,3,3,256,256]{4,3,2,1,0:T(8,128)(2,1)S(1)} %copy-d, ...), kind=kLoop, calls=%fused_computation.97 | loop fusion | bytes 7077888 | tf_op jit(solution)/shard_map/slice | solution.py:76
  36.1 1.9 %slice.131 = bf16[3,1,1,256,256]{4,3,2,1,0:T(8,128)(2,1)} reverse(bf16[3,1,1,256,256]{4,3,2,1,0:T(8,128)(2,1)} %get-tuple-element.7), dimensions={0} | reverse | bytes 786432 | tf_op jit(solution)/shard_map/slice | solution.py:76
  38.0 0.8 reduce_sum.112
  39.4 21.8 %all-to-all-start.1 = ((f32[4,1,64]{2,1,0:T(1,128)}), f32[4,1,64]{2,1,0:T(1,128)S(1)}, u32[]{:S(2)}, u32[]{:S(2)}) async-start(f32[4,1,64]{2,1,0:T(1,128)} %broadcast_in_dim.31), calls=%async_computation.1 | async-start | bytes 4096 | tf_op jit(solution)/shard_map/all_to_all | solution.py:35
  61.2 1.8 %slice.125 = bf16[3,1,1,256,256]{4,3,2,1,0:T(8,128)(2,1)} reverse(bf16[3,1,1,256,256]{4,3,2,1,0:T(8,128)(2,1)} %get-tuple-element.8), dimensions={0} | reverse | bytes 786432 | tf_op jit(solution)/shard_map/slice | solution.py:76
  63.0 1.8 %slice.122 = bf16[3,1,1,256,256]{4,3,2,1,0:T(8,128)(2,1)} reverse(bf16[3,1,1,256,256]{4,3,2,1,0:T(8,128)(2,1)} %get-tuple-element.9), dimensions={0} | reverse | bytes 786432 | tf_op jit(solution)/shard_map/slice | solution.py:76
  64.9 0.8 slice.119
  65.7 0.8 slice.114
  68.5 2.4 %fusion.34 = f32[4,424,256,1]{2,1,3,0:T(8,128)S(1)} fusion(bf16[1,4,424,256]{3,2,0,1:T(8,128)(2,1)} %bitcast.7, bf16[1,4,424,256]{3,2,0,1:T(8,128)(2,1)} %bitcast.6, bf16[1,4,424,256]{3,2,0,1:T(8,128)(2,1)S(1)} %bitcast.153, bf16[3,1,1,256,256]{4,3,2,1,0:T(8,128)(2,1)} %slice.119), kind=kOutput, calls=%fused_computation.38 | convolution fusion | flops 669499392 | bytes 4734976 | tf_op jit(solution)/shard_map/myxo,mco->yxc/dot_general | solution.py:73
  71.0 4.5 %select_maximum_fusion = bf16[3,6,426,256]{3,2,0,1:T(8,128)(2,1)S(1)} fusion(bf16[3,1,424,256]{3,2,0,1:T(8,128)(2,1)} %collective-permute-done.3, bf16[3,1,424,256]{3,2,0,1:T(8,128)(2,1)} %collective-permute-done.2, bf16[1,4,424,256]{3,2,0,1:T(8,128)(2,1)} %bitcast.7, bf16[1,4,424,256]{3,2,0,1:T(8,128)(2,1)} %bitcast.6, bf16[1,4,424,256]{3,2,0,1:T(8,128)(2,1)S(1)} %bitcast.154), kind=kLoop, calls=%fused_computation.3 | loop fusion | flops 35334144 | bytes 7833600 | tf_op jit(solution)/shard_map/concatenate | solution.py:29
  75.5 1.0 fusion.24
  76.5 0.9 fusion.26
  77.4 1.0 fusion.28
  78.4 0.9 fusion.30
  79.4 1.0 fusion.32
  80.4 2.4 %fusion.14 = f32[4,424,256,1]{2,1,3,0:T(8,128)S(1)} fusion(bf16[1,4,424,256]{3,2,0,1:T(8,128)(2,1)} %bitcast.7, bf16[1,4,424,256]{3,2,0,1:T(8,128)(2,1)} %bitcast.6, bf16[1,4,424,256]{3,2,0,1:T(8,128)(2,1)S(1)} %bitcast.155, bf16[3,1,424,256]{3,2,0,1:T(8,128)(2,1)} %collective-permute-done.2, bf16[3,1,1,256,256]{4,3,2,1,0:T(8,128)(2,1)S(1)} %copy-done.14), kind=kOutput, calls=%fused_computation.18 | convolution fusion | flops 679919616 | bytes 5386240 | tf_op jit(solution)/shard_map/myxo,mco->yxc/dot_general | solution.py:73
  82.8 2.5 %fusion.6 = f32[4,424,256,1]{2,1,3,0:T(8,128)S(1)} fusion(bf16[3,1,424,256]{3,2,0,1:T(8,128)(2,1)} %collective-permute-done.3, bf16[1,4,424,256]{3,2,0,1:T(8,128)(2,1)} %bitcast.7, bf16[1,4,424,256]{3,2,0,1:T(8,128)(2,1)} %bitcast.6, bf16[1,4,424,256]{3,2,0,1:T(8,128)(2,1)S(1)} %bitcast.156, bf16[3,1,1,256,256]{4,3,2,1,0:T(8,128)(2,1)S(1)} %slice.111), kind=kOutput, calls=%fused_computation.10 | convolution fusion | flops 679919616 | bytes 5386240 | tf_op jit(solution)/shard_map/myxo,mco->yxc/dot_general | solution.py:73
  85.3 2.1 %fusion.76 = (f32[256]{0:T(256)S(1)}, f32[256]{0:T(256)S(1)}, f32[4,424,256]{2,1,0:T(8,128)S(1)}) fusion(f32[256]{0:T(256)S(1)} %mul.60, f32[256]{0:T(256)S(1)} %sub.30, bf16[1,4,424,256]{3,2,1,0:T(8,128)(2,1)S(1)} %copy-done, f32[256]{0:T(256)S(1)} %copy-done.15, f32[256]{0:T(256)S(1)} %copy-done.16, bf16[3,1,1,256,256]{4,3,2,1,0:T(8,128)(2,1)S(1)} %copy-done.9, ...), kind=kOutput, calls=%fused_computation.96 | convolution fusion | flops 677748224 | bytes 19503104 | tf_op jit(solution)/shard_map/myxo,mco->yxc/dot_general | solution.py:73
  88.0 20.5 %all_to_all.24 = f32[64,1,64]{2,1,0:T(1,128)S(1)} all-to-all(f32[64,1,64]{2,1,0:T(1,128)S(1)} %broadcast_in_dim.34), channel_id=1, replica_groups=mesh['frames'=4,'rows_0'=4,'rows_1'=8,'rows_2'=2] {'rows_0','rows_1','ro..., dimensions={0} | all-to-all | bytes 32768 | tf_op jit(solution)/shard_map/all_to_all | solution.py:35
  108.5 8.1 %all_to_all.25 = f32[4,1,64]{2,1,0:T(1,128)S(1)} all-to-all(f32[4,1,64]{2,1,0:T(1,128)S(1)} %broadcast_in_dim.35), channel_id=1, replica_groups=mesh['frames'=4,'rows_0'=4,'rows_1'=8,'rows_2'=2] {'frames'}, dimensions={0} | all-to-all | bytes 2048 | tf_op jit(solution)/shard_map/all_to_all | solution.py:35
  117.1 1.3 %fusion.63 = bf16[1,4,424,256]{3,2,1,0:T(8,128)(2,1)} fusion(bf16[1,4,424,256]{3,2,1,0:T(8,128)(2,1)S(1)} %copy-done, f32[4,424,256]{2,1,0:T(8,128)S(1)} %get-tuple-element.22, f32[256]{0:T(256)S(1)} %mul.70, f32[256]{0:T(256)S(1)} %sub.34, f32[256]{0:T(256)S(1)} %sub.30, f32[256]{0:T(256)S(1)} %mul.60), kind=kLoop, calls=%fused_computation.75 | loop fusion | flops 3473408 | bytes 3477504 | tf_op jit(solution)/shard_map/broadcast_in_dim | solution.py:115
  (68 shorter events, 5.8 us)
Async XLA Ops:
  0.0 25.1 %collective-permute-start.1 = (bf16[4,424,256]{2,1,0:T(8,128)(2,1)}, bf16[4,424,256]{2,1,0:T(8,128)(2,1)}, u32[]{:S(2)}, u32[]{:S(2)}) collective-permute-start(bf16[4,424,256]{2,1,0:T(8,128)(2,1)} %bitcast.150), channel_id=1, source_target_pairs={{128,0},{192,64},{129,1},{193,65},{130,2},{194,66},{131,3},{195,67... | collective-permute-start | bytes 2605064 | tf_op jit(solution)/shard_map/ppermute | solution.py:17
  1.3 23.8 %collective-permute-start = (bf16[4,424,256]{2,1,0:T(8,128)(2,1)}, bf16[4,424,256]{2,1,0:T(8,128)(2,1)}, u32[]{:S(2)}, u32[]{:S(2)}) collective-permute-start(bf16[4,424,256]{2,1,0:T(8,128)(2,1)} %bitcast.151), channel_id=1, source_target_pairs={{64,0},{128,64},{192,128},{65,1},{129,65},{193,129},{66,2},{130,66... | collective-permute-start | bytes 2605064 | tf_op jit(solution)/shard_map/ppermute | solution.py:17
  4.6 29.6 %copy-start.1 = (bf16[3,3,3,256,256]{4,3,2,1,0:T(8,128)(2,1)S(1)}, bf16[3,3,3,256,256]{4,3,2,1,0:T(8,128)(2,1)}, u32[]{:S(2)}) copy-start(bf16[3,3,3,256,256]{4,3,2,1,0:T(8,128)(2,1)} %param.7) | copy-start | bytes 10616836
  11.9 26.1 %all-to-all-start = ((f32[64,1,64]{2,1,0:T(1,128)}), f32[64,1,64]{2,1,0:T(1,128)}, u32[]{:S(2)}, u32[]{:S(2)}) async-start(f32[64,1,64]{2,1,0:T(1,128)} %broadcast_in_dim.30), calls=%async_computation | async-start | bytes 65536 | tf_op jit(solution)/shard_map/all_to_all | solution.py:35
  27.7 43.2 %collective-permute-start.3 = (bf16[3,1,424,256]{3,2,0,1:T(8,128)(2,1)}, bf16[3,1,424,256]{3,2,0,1:T(8,128)(2,1)}, u32[]{:S(2)}, u32[]{:S(2)}) collective-permute-start(bf16[3,1,424,256]{3,2,0,1:T(8,128)(2,1)} %get-tuple-element.16), channel_id=1, source_target_pairs={{1,0},{2,1},{3,2},{4,3},{5,4},{6,5},{7,6},{8,7},{9,8},{10,9},{11,1... | collective-permute-start | bytes 1953800 | tf_op jit(solution)/shard_map/ppermute | solution.py:28
  30.4 40.6 %collective-permute-start.2 = (bf16[3,1,424,256]{3,2,0,1:T(8,128)(2,1)}, bf16[3,1,424,256]{3,2,0,1:T(8,128)(2,1)}, u32[]{:S(2)}, u32[]{:S(2)}) collective-permute-start(bf16[3,1,424,256]{3,2,0,1:T(8,128)(2,1)} %get-tuple-element.17), channel_id=1, source_target_pairs={{0,1},{1,2},{2,3},{3,4},{4,5},{5,6},{6,7},{7,8},{8,9},{9,10},{10,1... | collective-permute-start | bytes 1953800 | tf_op jit(solution)/shard_map/ppermute | solution.py:27
  36.1 28.8 %copy-start.8 = (bf16[3,1,1,256,256]{4,3,2,1,0:T(8,128)(2,1)S(1)}, bf16[3,1,1,256,256]{4,3,2,1,0:T(8,128)(2,1)}, u32[]{:S(2)}) copy-start(bf16[3,1,1,256,256]{4,3,2,1,0:T(8,128)(2,1)} %get-tuple-element.10) | copy-start | bytes 1179652
  36.1 29.6 %copy-start.7 = (bf16[3,1,1,256,256]{4,3,2,1,0:T(8,128)(2,1)S(1)}, bf16[3,1,1,256,256]{4,3,2,1,0:T(8,128)(2,1)}, u32[]{:S(2)}) copy-start(bf16[3,1,1,256,256]{4,3,2,1,0:T(8,128)(2,1)} %get-tuple-element.11) | copy-start | bytes 1179652
  36.1 29.6 %copy-start.6 = (bf16[3,1,1,256,256]{4,3,2,1,0:T(8,128)(2,1)S(1)}, bf16[3,1,1,256,256]{4,3,2,1,0:T(8,128)(2,1)}, u32[]{:S(2)}) copy-start(bf16[3,1,1,256,256]{4,3,2,1,0:T(8,128)(2,1)} %get-tuple-element.12) | copy-start | bytes 1179652
  36.1 30.4 %copy-start.5 = (bf16[3,1,1,256,256]{4,3,2,1,0:T(8,128)(2,1)S(1)}, bf16[3,1,1,256,256]{4,3,2,1,0:T(8,128)(2,1)}, u32[]{:S(2)}) copy-start(bf16[3,1,1,256,256]{4,3,2,1,0:T(8,128)(2,1)} %get-tuple-element.13) | copy-start | bytes 1179652
  36.1 30.4 %copy-start.4 = (bf16[3,1,1,256,256]{4,3,2,1,0:T(8,128)(2,1)S(1)}, bf16[3,1,1,256,256]{4,3,2,1,0:T(8,128)(2,1)}, u32[]{:S(2)}) copy-start(bf16[3,1,1,256,256]{4,3,2,1,0:T(8,128)(2,1)} %get-tuple-element.14) | copy-start | bytes 1179652
  39.4 28.7 %all-to-all-start.1 = ((f32[4,1,64]{2,1,0:T(1,128)}), f32[4,1,64]{2,1,0:T(1,128)S(1)}, u32[]{:S(2)}, u32[]{:S(2)}) async-start(f32[4,1,64]{2,1,0:T(1,128)} %broadcast_in_dim.31), calls=%async_computation.1 | async-start | bytes 4096 | tf_op jit(solution)/shard_map/all_to_all | solution.py:35
  61.2 6.1 %copy-start.3 = (bf16[3,1,1,256,256]{4,3,2,1,0:T(8,128)(2,1)S(1)}, bf16[3,1,1,256,256]{4,3,2,1,0:T(8,128)(2,1)}, u32[]{:S(2)}) copy-start(bf16[3,1,1,256,256]{4,3,2,1,0:T(8,128)(2,1)} %get-tuple-element.15) | copy-start | bytes 1179652
  63.0 5.5 %copy-start.2 = (bf16[1,4,424,256]{3,2,1,0:T(8,128)(2,1)S(1)}, bf16[1,4,424,256]{3,2,1,0:T(8,128)(2,1)}, u32[]{:S(2)}) copy-start(bf16[1,4,424,256]{3,2,1,0:T(8,128)(2,1)} %param.6) | copy-start | bytes 2605060
  70.9 4.5 %copy-start.10 = (bf16[3,1,1,256,256]{4,3,2,1,0:T(8,128)(2,1)S(1)}, bf16[3,1,1,256,256]{4,3,2,1,0:T(8,128)(2,1)}, u32[]{:S(2)}) copy-start(bf16[3,1,1,256,256]{4,3,2,1,0:T(8,128)(2,1)} %slice.125) | copy-start | bytes 1179652
  75.5 1.0 copy-start.11
  77.4 1.0 copy-start.12
  78.4 1.0 copy-start.13
  79.4 1.0 copy-start.14
  82.8 2.5 %copy-start = (bf16[1,4,424,256]{3,2,1,0:T(8,128)(2,1)S(1)}, bf16[1,4,424,256]{3,2,1,0:T(8,128)(2,1)}, u32[]{:S(2)}) copy-start(bf16[1,4,424,256]{3,2,1,0:T(8,128)(2,1)} %param.5) | copy-start | bytes 2605060
  82.8 2.5 %copy-start.9 = (bf16[3,1,1,256,256]{4,3,2,1,0:T(8,128)(2,1)S(1)}, bf16[3,1,1,256,256]{4,3,2,1,0:T(8,128)(2,1)}, u32[]{:S(2)}) copy-start(bf16[3,1,1,256,256]{4,3,2,1,0:T(8,128)(2,1)} %slice.131) | copy-start | bytes 1179652
  82.8 2.5 %copy-start.15 = (f32[256]{0:T(256)S(1)}, f32[256]{0:T(256)}, u32[]{:S(2)}) copy-start(f32[256]{0:T(256)} %param.9) | copy-start | bytes 3076
  82.8 2.5 %copy-start.16 = (f32[256]{0:T(256)S(1)}, f32[256]{0:T(256)}, u32[]{:S(2)}) copy-start(f32[256]{0:T(256)} %param.8) | copy-start | bytes 3076
where the time goes:
time: 119 us; the launch traced here: 118 us
  starting transfers between devices  44.1 us (37%)
  blocking collectives  28.7 us (24%)
  other arithmetic  16.2 us (14%)
  local copies, waits for them, and re-layouts  15.1 us (13%)
  matrix products  14.1 us (12%)
    all_to_all x2, starting transfers between devices, from_everyone(): return lax.all_to_all(copies, axis, split_axis=0, concat_axis=0, tiled=True)  35 us
    all_to_all x2, blocking collectives, from_everyone(): return lax.all_to_all(copies, axis, split_axis=0, concat_axis=0, tiled=True)  28.7 us
    dot_general x9, matrix products, transpose_conv(): jnp.einsum('myxo,mco->yxc', window, flipped[:, row_tap, col_tap], preferr...  14.1 us
    slice x10, local copies, waits for them, and re-layouts, transpose_conv(): flipped[:, row_tap, col_tap]  10.6 us
    concatenate x1, other arithmetic, padded_2(): value = jnp.concatenate([before, value, after], axis=dim)  4.5 us
    reduce_sum x2, other arithmetic, group_sum(): per_chan = jnp.sum(values, axis=(0, 1))  4.14 us
    ppermute x1, starting transfers between devices, padded_2(): before = lax.ppermute(last, axis, up)  3.81 us
    ppermute x1, starting transfers between devices, padded_2(): after = lax.ppermute(first, axis, down)  2.68 us
  transfers between devices with their start and end apart: 6, of which 0 were waited for; matrix products, arithmetic and copies ran while one was open for 23% of the time, Pallas kernels for 0%

commit v1 on v0

v1 whole, which is shorter than its diff:
```python
import functools

import jax
import jax.numpy as jnp
from jax import lax
from jax.experimental import pallas as pl
from jax.experimental.pallas import tpu as pltpu
from jax.sharding import PartitionSpec as P

GROUPS = 32
EPS = 1e-06
MESH = pl.DeviceIdType.MESH
FRAMES, STRIPS = 4, 64
PAD = 8


def plane_peers(f, r):
    out = []
    for dy in range(4):
        for dx in range(4):
            if dy or dx:
                out.append((lax.rem(f + dy, 4), lax.rem(r + 16 * dx, 64)))
    return out


def line_peers(f, r):
    base, low = 16 * (r // 16), lax.rem(r, 16)
    return [(f, base + lax.rem(low + d, 16)) for d in range(1, 16)]


def over_group(total, channels):
    lane = lax.broadcasted_iota(jnp.int32, total.shape, 1)
    step = 1
    while step < channels // GROUPS:
        up = pltpu.roll(total, channels - step, 1)
        down = pltpu.roll(total, step, 1)
        total = total + jnp.where((lane // step) % 2 == 0, up, down)
        step *= 2
    return total


def body(
    cells_per, x_hbm, cot_hbm, k_hbm, gain_ref, bias_ref, g_ref, stat_ref,
    xin, cot, weights, acc, slope, cur, near, far,
    lsem, own_send, frame_recv, relay_send, halo_send, halo_recv, ar_send, ar_recv,
):
    f, r = lax.axis_index("frames"), lax.axis_index("rows")
    rows, width, channels = xin.shape
    half = channels // 2
    slots = 3 - (f // 2) * (f - 1)

    load_cot = pltpu.make_async_copy(cot_hbm.at[0], cot.at[0, pl.ds(1, rows)], lsem.at[0])
    load_x = pltpu.make_async_copy(x_hbm.at[0], xin, lsem.at[1])
    load_k = pltpu.make_async_copy(k_hbm, weights, lsem.at[2])
    load_cot.start()
    load_x.start()
    load_k.start()

    barrier = pltpu.get_barrier_semaphore()
    greeted = plane_peers(f, r) + line_peers(f, r)
    greeted += [(f, lax.rem(r + 1, STRIPS)), (f, lax.rem(r + STRIPS - 1, STRIPS))]
    for peer in greeted:
        pl.semaphore_signal(barrier, inc=1, device_id=peer, device_id_type=MESH)

    acc[...] = jnp.zeros_like(acc)
    load_x.wait()

    def add_stats(y, carry):
        values = xin[y].astype(jnp.float32)
        return (
            carry[0] + jnp.sum(values, axis=0, keepdims=True),
            carry[1] + jnp.sum(values * values, axis=0, keepdims=True),
        )

    zero = jnp.zeros((1, channels), jnp.float32)
    first, second = lax.fori_loop(0, rows, add_stats, (zero, zero))
    load_cot.wait()
    pl.semaphore_wait(barrier, len(greeted))

    def piece(slot, row, h):
        return cot.at[slot, row, :, pl.ds(h * half, half)]

    def own_copy(q, h):
        row, slot = 1 + lax.rem(3 * q, 4), 2 - lax.rem(f, 2)
        return pltpu.make_async_remote_copy(
            piece(0, row, h), piece(slot, row, h), own_send.at[q, h],
            frame_recv.at[slot - 1, q, h], device_id=((f // 3) * 2, r), device_id_type=MESH,
        )

    def relay_copy(q, h):
        row, source, slot = 1 + lax.rem(3 * q, 4), 2 - f // 2, 1 + f // 2
        return pltpu.make_async_remote_copy(
            piece(source, row, h), piece(slot, row, h), relay_send.at[q, h],
            frame_recv.at[slot - 1, q, h], device_id=(1, r), device_id_type=MESH,
        )

    def await_piece(slot, q, h):
        row = 1 + lax.rem(3 * q, 4)
        pltpu.make_async_remote_copy(
            piece(slot, row, h), piece(slot, row, h), own_send.at[q, h],
            frame_recv.at[slot - 1, q, h], device_id=(f, r), device_id_type=MESH,
        ).wait_recv()

    def halo_up(a):
        return pltpu.make_async_remote_copy(
            cot.at[a, 1], cot.at[a, rows + 1], halo_send.at[a, 0], halo_recv.at[a, 0],
            device_id=(f, lax.rem(r + STRIPS - 1, STRIPS)), device_id_type=MESH,
        )

    def halo_down(a):
        return pltpu.make_async_remote_copy(
            cot.at[a, rows], cot.at[a, 0], halo_send.at[a, 1], halo_recv.at[a, 1],
            device_id=(f, lax.rem(r + 1, STRIPS)), device_id_type=MESH,
        )

    @pl.when(f > 0)
    def _():
        for q in range(4):
            for h in range(2):
                own_copy(q, h).start()

    @pl.when(r > 0)
    def _():
        halo_up(0).start()

    @pl.when(r < STRIPS - 1)
    def _():
        halo_down(0).start()

    def send_stage(k, peers, slots_ref):
        for j, peer in enumerate(peers):
            pltpu.make_async_remote_copy(
                cur.at[k], slots_ref.at[j], ar_send.at[k], ar_recv.at[k],
                device_id=peer, device_id_type=MESH,
            ).start()

    def whole_stage(k, slots_ref):
        return pltpu.make_async_remote_copy(
            slots_ref, slots_ref, ar_send.at[k], ar_recv.at[k],
            device_id=(f, r), device_id_type=MESH,
        )

    def end_stage(k, slots_ref):
        whole_stage(k, slots_ref).wait_recv()
        return cur[k] + jnp.sum(slots_ref[...], axis=0)

    cur[0] = jnp.concatenate([first, second], axis=0)
    send_stage(0, plane_peers(f, r), near.at[0])

    def add_row(a, row):
        def tap(b, carry):
            y = row - b

            @pl.when((y >= 0) & (y < rows))
            def _():
                acc[y, pl.ds(PAD, width), :] += lax.dot_general(
                    cot[a, row], weights[2 - a, 2 - b], (((1,), (1,)), ((), ())),
                    preferred_element_type=jnp.float32,
                )
            return carry

        lax.fori_loop(0, 3, tap, 0)

    def add_halos(a, carry):
        @pl.when(r > 0)
        def _():
            halo_down(a).wait_recv()

        @pl.when(r < STRIPS - 1)
        def _():
            halo_up(a).wait_recv()

        def edge(e, c):
            @pl.when(((e == 0) & (r > 0)) | ((e == 1) & (r < STRIPS - 1)))
            def _():
                add_row(a, e * (rows + 1))
            return c

        lax.fori_loop(0, 2, edge, 0)
        return carry

    load_k.wait()

    def own_row(i, carry):
        add_row(0, i + 1)
        return carry

    lax.fori_loop(0, rows, own_row, 0)

    def wave(q, carry):
        row = 1 + lax.rem(3 * q, 4)

        @pl.when(q == 3)
        def _():
            lax.fori_loop(0, slots, add_halos, 0)

        for h in range(2):
            @pl.when((f == 0) | (f == 2))
            def _(h=h):
                await_piece(2 - f // 2, q, h)
                relay_copy(q, h).start()

        for h in range(2):
            @pl.when(f < 2)
            def _(h=h):
                await_piece(1, q, h)

            @pl.when(f == 1)
            def _(h=h):
                await_piece(2, q, h)

        def send_halo(a, c):
            @pl.when((q == 0) & (r > 0))
            def _():
                halo_up(a).start()

            @pl.when((q == 1) & (r < STRIPS - 1))
            def _():
                halo_down(a).start()
            return c

        def slot_row(a, c):
            add_row(a, row)
            return c

        lax.fori_loop(1, slots, send_halo, 0)
        lax.fori_loop(1, slots, slot_row, 0)

        @pl.when(q == 0)
        def _():
            cur[1] = end_stage(0, near.at[0])
            send_stage(1, line_peers(f, r), far.at[0])

        @pl.when(q == 1)
        def _():
            total = over_group(end_stage(1, far.at[0]), channels) / cells_per
            centre = total[0:1]
            variance = jnp.maximum(total[1:2] - centre * centre, 0.0)
            stat_ref[0:1] = centre
            stat_ref[1:2] = lax.rsqrt(variance + EPS)

        @pl.when(q == 2)
        def _():
            def slope_row(y, c):
                normed = (xin[y].astype(jnp.float32) - stat_ref[0:1]) * stat_ref[1:2]
                preact = normed * gain_ref[...] + bias_ref[...]
                logistic = jax.nn.sigmoid(preact)
                slope[y] = logistic * (1.0 + preact * (1.0 - logistic)) * gain_ref[...]
                return c

            lax.fori_loop(0, rows, slope_row, 0)

        return carry

    lax.fori_loop(0, 4, wave, 0)

    def grad_row(y, carry):
        act_grad = (
            acc[y, pl.ds(PAD + 1, width), 0:channels]
            + acc[y, pl.ds(PAD, width), channels : 2 * channels]
            + acc[y, pl.ds(PAD - 1, width), 2 * channels : 3 * channels]
        )
        norm_grad = act_grad * slope[y]
        g_ref[y] = norm_grad
        normed = (xin[y].astype(jnp.float32) - stat_ref[0:1]) * stat_ref[1:2]
        return (
            carry[0] + jnp.sum(norm_grad, axis=0, keepdims=True),
            carry[1] + jnp.sum(norm_grad * normed, axis=0, keepdims=True),
        )

    first, second = lax.fori_loop(0, rows, grad_row, (zero, zero))
    cur[2] = jnp.concatenate([first, second], axis=0)
    send_stage(2, plane_peers(f, r), near.at[1])
    cur[3] = end_stage(2, near.at[1])
    send_stage(3, line_peers(f, r), far.at[1])

    @pl.when(f > 0)
    def _():
        for q in range(4):
            for h in range(2):
                own_copy(q, h).wait_send()

    @pl.when((f == 0) | (f == 2))
    def _():
        for q in range(4):
            for h in range(2):
                relay_copy(q, h).wait_send()

    def halo_sent(a, c):
        @pl.when(r > 0)
        def _():
            halo_up(a).wait_send()

        @pl.when(r < STRIPS - 1)
        def _():
            halo_down(a).wait_send()
        return c

    lax.fori_loop(0, slots, halo_sent, 0)
    total = over_group(end_stage(3, far.at[1]), channels) / cells_per
    stat_ref[2:4] = total
    for k, slots_ref in enumerate((near.at[0], far.at[0], near.at[1], far.at[1])):
        whole_stage(k, slots_ref).wait_send()


def shards(inputs, cotangent, kernel, norm_gain, norm_bias):
    _, rows, width, channels = inputs.shape
    cells_per = FRAMES * STRIPS * rows * width * (channels // GROUPS)
    vmem, anywhere = pl.BlockSpec(memory_space=pltpu.VMEM), pl.BlockSpec(memory_space=pl.ANY)
    dma = pltpu.SemaphoreType.DMA
    norm_grad, stats = pl.pallas_call(
        functools.partial(body, cells_per),
        out_shape=(
            jax.ShapeDtypeStruct((rows, width, channels), jnp.float32),
            jax.ShapeDtypeStruct((4, channels), jnp.float32),
        ),
        in_specs=[anywhere, anywhere, anywhere, vmem, vmem],
        out_specs=(vmem, vmem),
        scratch_shapes=[
            pltpu.VMEM((rows, width, channels), jnp.bfloat16),
            pltpu.VMEM((3, rows + 2, width, channels), jnp.bfloat16),
            pltpu.VMEM((3, 3, 3 * channels, channels), jnp.bfloat16),
            pltpu.VMEM((rows, width + 2 * PAD, 3 * channels), jnp.float32),
            pltpu.VMEM((rows, width, channels), jnp.float32),
            pltpu.VMEM((4, 2, channels), jnp.float32),
            pltpu.VMEM((2, 15, 2, channels), jnp.float32),
            pltpu.VMEM((2, 15, 2, channels), jnp.float32),
            dma((3,)), dma((4, 2)), dma((2, 4, 2)), dma((4, 2)),
            dma((3, 2)), dma((3, 2)), dma((4,)), dma((4,)),
        ],
        compiler_params=pltpu.CompilerParams(
            collective_id=0, has_side_effects=True, vmem_limit_bytes=48 << 20
        ),
    )(
        inputs, cotangent, kernel.reshape(3, 3, 3 * channels, channels),
        norm_gain[None], norm_bias[None],
    )
    normed = (inputs[0].astype(jnp.float32) - stats[0]) * stats[1]
    input_grad = stats[1] * (norm_grad - stats[2] - normed * stats[3])
    return input_grad.astype(jnp.bfloat16)[None]


def solution(mesh):
    placed = P("frames", "rows", None, None)
    return jax.shard_map(
        shards, mesh=mesh, in_specs=(placed, placed, P(), P(), P()), out_specs=placed, check_vma=False
    )
```

time: 119 us -> 69.3 us (0.58)
  Pallas kernels: 0 us -> 64 us
  starting transfers between devices: 44.1 us -> 0 us
  blocking collectives: 28.7 us -> 0 us
  other arithmetic: 16.2 us -> 1.38 us
  matrix products: 14.1 us -> 0 us
  local copies, waits for them, and re-layouts: 15.1 us -> 3.69 us
    pallas_call x0 -> x1, Pallas kernels: none -> 64 us  [shards(): pl.pallas_call(functools.partial(body, cells_per), out_shape=(jax.ShapeDt...]
    all_to_all x2 -> x0, starting transfers between devices: 35 us -> none  [from_everyone(): return lax.all_to_all(copies, axis, split_axis=0, concat_axis=0, tiled=True)]
    all_to_all x2 -> x0, blocking collectives: 28.7 us -> none  [from_everyone(): return lax.all_to_all(copies, axis, split_axis=0, concat_axis=0, tiled=True)]
    dot_general x9 -> x0, matrix products: 14.1 us -> none  [transpose_conv(): jnp.einsum('myxo,mco->yxc', window, flipped[:, row_tap, col_tap], preferr...]
    slice x10 -> x1, local copies, waits for them, and re-layouts: 10.6 us -> 0.01 us  [shards(): input_grad = stats[1] * (norm_grad - stats[2] - normed * stats[3])]
    ppermute x4 -> x0, starting transfers between devices: 9.06 us -> none  [the longest x1 3.81 us: padded_2(): before = lax.ppermute(last, axis, up)]
    reduce_sum x10 -> x0, other arithmetic: 6.76 us -> none  [the longest x2 4.14 us: group_sum(): per_chan = jnp.sum(values, axis=(0, 1))]
    concatenate x3 -> x0, other arithmetic: 5.32 us -> none  [the longest x1 4.5 us: padded_2(): value = jnp.concatenate([before, value, after], axis=dim)]
  transfers between devices with their start and end apart: 6 -> 0, of which waited for: 0 -> 0; matrix products, arithmetic and copies ran while one was open for 23% -> 0% of each run, Pallas kernels for 0% -> 0%
where the time goes in v1:
time: 69.3 us; the launch traced here: 69.1 us
  Pallas kernels  64 us (92%)
  local copies, waits for them, and re-layouts  3.69 us (5%)
  other arithmetic  1.38 us (2%)
    pallas_call x1, Pallas kernels, shards(): pl.pallas_call(functools.partial(body, cells_per), out_shape=(jax.ShapeDt...  64 us
    unnamed x8, local copies, waits for them, and re-layouts  3.68 us

profile of v1, /device:TPU:1, one launch (start us, length us, event | category | flops | bytes accessed | tf_op | source)
XLA Modules:
  0.0 69.1 jit_solution(9525779339357622788)
XLA Ops:
  0.0 0.0 copy-start
  0.0 1.2 %copy-done = bf16[1,4,424,256]{3,2,1,0:T(8,128)(2,1)S(1)} copy-done((bf16[1,4,424,256]{3,2,1,0:T(8,128)(2,1)S(1)}, bf16[1,4,424,256]{3,2,1,0:T(8,128)(2,1)}, u32[]{:S(2)}) %copy-start) | copy-done | bytes 868376
  1.2 0.0 copy-start.1
  1.2 1.2 %copy-done.1 = bf16[1,4,424,256]{3,2,1,0:T(8,128)(2,1)S(1)} copy-done((bf16[1,4,424,256]{3,2,1,0:T(8,128)(2,1)S(1)}, bf16[1,4,424,256]{3,2,1,0:T(8,128)(2,1)}, u32[]{:S(2)}) %copy-start.1) | copy-done | bytes 868376
  2.3 0.0 copy-start.2
  2.3 0.7 copy-done.2
  3.0 0.0 copy-start.3
  3.0 0.7 copy-done.3
  3.7 64.0 %shard_map.55 = (f32[4,424,256]{2,1,0:T(8,128)S(1)}, f32[4,256]{1,0:T(4,128)S(1)}) custom-call(bf16[1,4,424,256]{3,2,1,0:T(8,128)(2,1)S(1)} %copy-done, bf16[1,4,424,256]{3,2,1,0:T(8,128)(2,1)S(1)} %copy-done.1, bf16[3,3,768,256]{3,2,1,0:T(8,128)(2,1)} %bitcast.14, f32[1,256]{1,0:T(1,128)S(1)} %bitcast.12, f32[1,256]{1,0:T(1,128)S(1)} %bitcast.13), custom_call_target="tpu_custom_call" | custom-call | tf_op jit(solution)/shard_map/pallas_call | solution.py:311
  67.7 1.4 %fusion.5 = bf16[1,4,424,256]{3,2,1,0:T(8,128)(2,1)} fusion(f32[4,424,256]{2,1,0:T(8,128)S(1)} %get-tuple-element.8, bf16[1,4,424,256]{3,2,1,0:T(8,128)(2,1)S(1)} %copy-done, f32[256]{0:T(256)S(1)} %bitcast.16, f32[256]{0:T(256)S(1)} %bitcast.17, f32[256]{0:T(256)S(1)} %bitcast.18, f32[256]{0:T(256)S(1)} %bitcast.15), kind=kLoop, calls=%fused_computation.6 | loop fusion | flops 3473408 | bytes 3477504 | tf_op jit(solution)/shard_map/broadcast_in_dim | solution.py:340
  (1 shorter events, 0.0 us)
Async XLA Ops:
  0.0 1.2 %copy-start = (bf16[1,4,424,256]{3,2,1,0:T(8,128)(2,1)S(1)}, bf16[1,4,424,256]{3,2,1,0:T(8,128)(2,1)}, u32[]{:S(2)}) copy-start(bf16[1,4,424,256]{3,2,1,0:T(8,128)(2,1)} %x_hbm.1) | copy-start | bytes 2605060
  1.2 1.2 %copy-start.1 = (bf16[1,4,424,256]{3,2,1,0:T(8,128)(2,1)S(1)}, bf16[1,4,424,256]{3,2,1,0:T(8,128)(2,1)}, u32[]{:S(2)}) copy-start(bf16[1,4,424,256]{3,2,1,0:T(8,128)(2,1)} %cot_hbm.1) | copy-start | bytes 2605060
  2.3 0.7 copy-start.2
  3.0 0.7 copy-start.3

commit v2 on v1

v2 whole, which is shorter than its diff:
```python
import functools

import jax
import jax.numpy as jnp
from jax import lax
from jax.experimental import pallas as pl
from jax.experimental.pallas import tpu as pltpu
from jax.sharding import PartitionSpec as P

GROUPS = 32
EPS = 1e-06
MESH = pl.DeviceIdType.MESH
FRAMES, STRIPS = 4, 64
PAD = 8


def plane_peers(f, r):
    out = []
    for dy in range(4):
        for dx in range(4):
            if dy or dx:
                out.append((lax.rem(f + dy, 4), lax.rem(r + 16 * dx, 64)))
    return out


def line_peers(f, r):
    base, low = 16 * (r // 16), lax.rem(r, 16)
    return [(f, base + lax.rem(low + d, 16)) for d in range(1, 16)]


def over_group(total, channels):
    lane = lax.broadcasted_iota(jnp.int32, total.shape, 1)
    step = 1
    while step < channels // GROUPS:
        up = pltpu.roll(total, channels - step, 1)
        down = pltpu.roll(total, step, 1)
        total = total + jnp.where((lane // step) % 2 == 0, up, down)
        step *= 2
    return total


def body(
    cells_per, x_hbm, cot_hbm, k_hbm, gain_hbm, bias_hbm, g_ref, stat_ref,
    xin, gain_ref, bias_ref, staged, cot, weights, acc, slope, cur, near, far,
    lsem, ksem, own_send, frame_recv, relay_send, halo_send, halo_recv, ar_send, ar_recv,
):
    f, r = lax.axis_index("frames"), lax.axis_index("rows")
    rows, width, channels = xin.shape
    half = channels // 2
    slots = 3 - (f // 2) * (f - 1)

    def load_weights(k):
        return pltpu.make_async_copy(k_hbm.at[k], weights.at[k], ksem.at[k])

    load_cot = pltpu.make_async_copy(cot_hbm.at[0], staged, lsem.at[0])

    load_x = pltpu.make_async_copy(x_hbm.at[0], xin, lsem.at[2])
    load_gain = pltpu.make_async_copy(gain_hbm, gain_ref, lsem.at[3])
    load_bias = pltpu.make_async_copy(bias_hbm, bias_ref, lsem.at[4])
    load_x.start()
    load_cot.start()
    for k in (2, 1, 0):
        load_weights(k).start()
    load_gain.start()
    load_bias.start()

    barrier = pltpu.get_barrier_semaphore()
    greeted = plane_peers(f, r) + line_peers(f, r)
    greeted += [(f, lax.rem(r + 1, STRIPS)), (f, lax.rem(r + STRIPS - 1, STRIPS))]
    for peer in greeted:
        pl.semaphore_signal(barrier, inc=1, device_id=peer, device_id_type=MESH)

    load_x.wait()

    def add_stats(y, carry):
        values = xin[y].astype(jnp.float32)
        return (
            carry[0] + jnp.sum(values, axis=0, keepdims=True),
            carry[1] + jnp.sum(values * values, axis=0, keepdims=True),
        )

    zero = jnp.zeros((1, channels), jnp.float32)
    first, second = lax.fori_loop(0, rows, add_stats, (zero, zero))
    cur[0] = jnp.concatenate([first, second], axis=0)

    def contract(left, right):
        return lax.dot_general(
            left, right, (((1,), (1,)), ((), ())), preferred_element_type=jnp.float32
        )

    def row_of(p):
        return 1 + lax.rem(3 * (p // 2), 4)

    def piece(slot, p):
        return cot.at[slot, row_of(p), lax.rem(p, 2)]

    def own_copy(p):
        slot = 2 - lax.rem(f, 2)
        return pltpu.make_async_remote_copy(
            cot_hbm.at[0, row_of(p) - 1, :, pl.ds(pl.multiple_of(lax.rem(p, 2) * half, half), half)],
            piece(slot, p), own_send.at[p], frame_recv.at[slot - 1, p],
            device_id=((f // 3) * 2, r), device_id_type=MESH,
        )

    def relay_copy(p):
        source, slot = 2 - f // 2, 1 + f // 2
        return pltpu.make_async_remote_copy(
            piece(source, p), piece(slot, p), relay_send.at[p], frame_recv.at[slot - 1, p],
            device_id=(1, r), device_id_type=MESH,
        )

    def await_piece(slot, p):
        pltpu.make_async_remote_copy(
            piece(slot, p), piece(slot, p), own_send.at[p], frame_recv.at[slot - 1, p],
            device_id=(f, r), device_id_type=MESH,
        ).wait_recv()

    def halo_up(a):
        return pltpu.make_async_remote_copy(
            cot.at[a, 1], cot.at[a, rows + 1], halo_send.at[a, 0], halo_recv.at[a, 0],
            device_id=(f, lax.rem(r + STRIPS - 1, STRIPS)), device_id_type=MESH,
        )

    def halo_down(a):
        return pltpu.make_async_remote_copy(
            cot.at[a, rows], cot.at[a, 0], halo_send.at[a, 1], halo_recv.at[a, 1],
            device_id=(f, lax.rem(r + 1, STRIPS)), device_id_type=MESH,
        )

    def send_stage(k, peers, slots_ref):
        for j, peer in enumerate(peers):
            pltpu.make_async_remote_copy(
                cur.at[k], slots_ref.at[j], ar_send.at[k], ar_recv.at[k],
                device_id=peer, device_id_type=MESH,
            ).start()

    def whole_stage(k, slots_ref):
        return pltpu.make_async_remote_copy(
            slots_ref, slots_ref, ar_send.at[k], ar_recv.at[k],
            device_id=(f, r), device_id_type=MESH,
        )

    def end_stage(k, slots_ref):
        whole_stage(k, slots_ref).wait_recv()
        return cur[k] + jnp.sum(slots_ref[...], axis=0)

    def both_frames(i, h):
        lanes = pl.ds(pl.multiple_of(h * half, half), half)
        return jnp.concatenate([weights[1, i, :, lanes], weights[0, i, :, lanes]], axis=-1)

    def add_piece(row, h):
        def tap(b, carry):
            y = row - b

            @pl.when((y >= 0) & (y < rows))
            def _():
                acc[y, pl.ds(PAD, width), :] += contract(
                    jnp.concatenate([cot[1, row, h], cot[2, row, h]], axis=-1),
                    both_frames(2 - b, h),
                )
            return carry

        lax.fori_loop(0, 3, tap, 0)

    def await_halo(a, e):
        @pl.when((e == 0) & (r > 0))
        def _():
            halo_down(a).wait_recv()

        @pl.when((e == 1) & (r < STRIPS - 1))
        def _():
            halo_up(a).wait_recv()

    blank = jnp.zeros((2, width, half), jnp.bfloat16)

    @pl.when(r == 0)
    def _():
        for a in range(3):
            cot[a, 0] = blank

    @pl.when(r == STRIPS - 1)
    def _():
        for a in range(3):
            cot[a, rows + 1] = blank

    @pl.when(f == 2)
    def _():
        def clear(row, carry):
            cot[2, row] = blank
            return carry

        lax.fori_loop(0, rows + 2, clear, 0)

    load_cot.wait()

    def split_row(y, carry):
        for h in range(2):
            cot[0, y + 1, h] = staged[y, :, h * half : (h + 1) * half]
        return carry

    lax.fori_loop(0, rows, split_row, 0)
    pl.semaphore_wait(barrier, len(greeted))
    send_stage(0, plane_peers(f, r), near.at[0])

    def send_own(p, carry):
        own_copy(p).start()
        return carry

    ahead = 8 - 4 * lax.rem(f + 1, 2)

    @pl.when(f > 0)
    def _():
        lax.fori_loop(0, ahead, send_own, 0)

    @pl.when(r > 0)
    def _():
        halo_up(0).start()

    @pl.when(r < STRIPS - 1)
    def _():
        halo_down(0).start()

    edge_rows = jnp.zeros((rows, PAD, 3 * channels), jnp.float32)
    acc[:, 0:PAD, :] = edge_rows
    acc[:, PAD + width :, :] = edge_rows
    load_weights(2).wait()
    for b in (1, 0, 2):
        low, high = max(b, 1), min(b + rows, rows + 1)
        block = staged[low - 1 : high - 1]
        product = contract(
            block.reshape((high - low) * width, channels), weights[2, 2 - b]
        ).reshape(high - low, width, 3 * channels)
        if b == 1:
            acc[:, pl.ds(PAD, width), :] = product
        else:
            acc[low - b : high - b, pl.ds(PAD, width), :] += product

    for k in (1, 0):
        load_weights(k).wait()
    load_gain.wait()
    load_bias.wait()

    def wave(p, carry):
        row, h = row_of(p), lax.rem(p, 2)

        @pl.when(f > 0)
        def _():
            @pl.when(p + ahead < 8)
            def _():
                own_copy(p).wait_send()
                own_copy(p + ahead).start()

        @pl.when((f == 0) | (f == 2))
        def _():
            await_piece(2 - f // 2, p)
            relay_copy(p).start()

        @pl.when(f < 2)
        def _():
            await_piece(1, p)

        @pl.when(f == 1)
        def _():
            await_piece(2, p)

        def send_halo(a, c):
            @pl.when((p == 1) & (r > 0))
            def _():
                halo_up(a).start()

            @pl.when((p == 3) & (r < STRIPS - 1))
            def _():
                halo_down(a).start()
            return c

        lax.fori_loop(1, slots, send_halo, 0)

        @pl.when(f < 3)
        def _():
            add_piece(row, h)

        @pl.when((p == 4) | (p == 6))
        def _():
            e = (p - 4) // 2

            def wait_slot(a, c):
                await_halo(a, e)
                return c

            lax.fori_loop(1, slots, wait_slot, 0)

            @pl.when(f < 3)
            def _():
                def halo_half(h2, c):
                    y = e * (rows - 1)
                    acc[y, pl.ds(PAD, width), :] += contract(
                        jnp.concatenate([cot[1, y + 2 * e, h2], cot[2, y + 2 * e, h2]], axis=-1),
                        both_frames(2 - 2 * e, h2),
                    )
                    return c

                lax.fori_loop(0, 2, halo_half, 0)

        @pl.when(p == 1)
        def _():
            cur[1] = end_stage(0, near.at[0])
            send_stage(1, line_peers(f, r), far.at[0])

        @pl.when(p == 3)
        def _():
            def own_halo(e, c):
                await_halo(0, e)
                y = e * (rows - 1)
                acc[y, pl.ds(PAD, width), :] += contract(
                    jnp.concatenate([cot[0, y + 2 * e, 0], cot[0, y + 2 * e, 1]], axis=-1),
                    weights[2, 2 - 2 * e],
                )
                return c

            lax.fori_loop(0, 2, own_halo, 0)

        @pl.when(p == 4)
        def _():
            total = over_group(end_stage(1, far.at[0]), channels) / cells_per
            centre = total[0:1]
            variance = jnp.maximum(total[1:2] - centre * centre, 0.0)
            stat_ref[0:1] = centre
            stat_ref[1:2] = lax.rsqrt(variance + EPS)

            def slope_row(y, c):
                normed = (xin[y].astype(jnp.float32) - stat_ref[0:1]) * stat_ref[1:2]
                preact = normed * gain_ref[...] + bias_ref[...]
                logistic = jax.nn.sigmoid(preact)
                slope[y] = logistic * (1.0 + preact * (1.0 - logistic)) * gain_ref[...]
                return c

            lax.fori_loop(0, rows, slope_row, 0)

        return carry

    lax.fori_loop(0, 8, wave, 0)

    def grad_row(y, carry):
        act_grad = (
            acc[y, pl.ds(PAD + 1, width), 0:channels]
            + acc[y, pl.ds(PAD, width), channels : 2 * channels]
            + acc[y, pl.ds(PAD - 1, width), 2 * channels : 3 * channels]
        )
        norm_grad = act_grad * slope[y]
        g_ref[y] = norm_grad
        normed = (xin[y].astype(jnp.float32) - stat_ref[0:1]) * stat_ref[1:2]
        return (
            carry[0] + jnp.sum(norm_grad, axis=0, keepdims=True),
            carry[1] + jnp.sum(norm_grad * normed, axis=0, keepdims=True),
        )

    first, second = lax.fori_loop(0, rows, grad_row, (zero, zero))
    cur[2] = jnp.concatenate([first, second], axis=0)
    send_stage(2, plane_peers(f, r), near.at[1])
    cur[3] = end_stage(2, near.at[1])
    send_stage(3, line_peers(f, r), far.at[1])

    @pl.when(f > 0)
    def _():
        def own_sent(p, c):
            own_copy(p).wait_send()
            return c

        lax.fori_loop(8 - ahead, 8, own_sent, 0)

    @pl.when((f == 0) | (f == 2))
    def _():
        def sent(p, c):
            relay_copy(p).wait_send()
            return c

        lax.fori_loop(0, 8, sent, 0)

    def halo_sent(a, c):
        @pl.when(r > 0)
        def _():
            halo_up(a).wait_send()

        @pl.when(r < STRIPS - 1)
        def _():
            halo_down(a).wait_send()
        return c

    lax.fori_loop(0, slots, halo_sent, 0)
    total = over_group(end_stage(3, far.at[1]), channels) / cells_per
    stat_ref[2:4] = total
    for k, slots_ref in enumerate((near.at[0], far.at[0], near.at[1], far.at[1])):
        whole_stage(k, slots_ref).wait_send()


def shards(inputs, cotangent, kernel, norm_gain, norm_bias):
    _, rows, width, channels = inputs.shape
    cells_per = FRAMES * STRIPS * rows * width * (channels // GROUPS)
    vmem, anywhere = pl.BlockSpec(memory_space=pltpu.VMEM), pl.BlockSpec(memory_space=pltpu.HBM)
    dma = pltpu.SemaphoreType.DMA
    norm_grad, stats = pl.pallas_call(
        functools.partial(body, cells_per),
        out_shape=(
            jax.ShapeDtypeStruct((rows, width, channels), jnp.float32),
            jax.ShapeDtypeStruct((4, channels), jnp.float32),
        ),
        in_specs=[anywhere] * 5,
        out_specs=(vmem, vmem),
        scratch_shapes=[
            pltpu.VMEM((rows, width, channels), jnp.bfloat16),
            pltpu.VMEM((1, channels), jnp.float32),
            pltpu.VMEM((1, channels), jnp.float32),
            pltpu.VMEM((rows, width, channels), jnp.bfloat16),
            pltpu.VMEM((3, rows + 2, 2, width, channels // 2), jnp.bfloat16),
            pltpu.VMEM((3, 3, 3 * channels, channels), jnp.bfloat16),
            pltpu.VMEM((rows, width + 2 * PAD, 3 * channels), jnp.float32),
            pltpu.VMEM((rows, width, channels), jnp.float32),
            pltpu.VMEM((4, 2, channels), jnp.float32),
            pltpu.VMEM((2, 15, 2, channels), jnp.float32),
            pltpu.VMEM((2, 15, 2, channels), jnp.float32),
            dma((5,)), dma((3,)), dma((8,)), dma((2, 8)), dma((8,)),
            dma((3, 2)), dma((3, 2)), dma((4,)), dma((4,)),
        ],
        compiler_params=pltpu.CompilerParams(
            collective_id=0, has_side_effects=True, vmem_limit_bytes=61 << 20
        ),
    )(
        inputs, cotangent, kernel.reshape(3, 3, 3 * channels, channels),
        norm_gain[None], norm_bias[None],
    )
    normed = (inputs[0].astype(jnp.float32) - stats[0]) * stats[1]
    input_grad = stats[1] * (norm_grad - stats[2] - normed * stats[3])
    return input_grad.astype(jnp.bfloat16)[None]


def solution(mesh):
    placed = P("frames", "rows", None, None)
    return jax.shard_map(
        shards, mesh=mesh, in_specs=(placed, placed, P(), P(), P()), out_specs=placed, check_vma=False
    )
```

time: 69.3 us -> 56.5 us (0.82)
  Pallas kernels: 64 us -> 52.7 us
  local copies, waits for them, and re-layouts: 3.69 us -> 0.82 us
  other arithmetic: 1.38 us -> 2.8 us
    pallas_call x1, Pallas kernels: 64 us -> 52.7 us  [shards(): pl.pallas_call(functools.partial(body, cells_per), out_shape=(jax.ShapeDt...]
    unnamed x8 -> x2, local copies, waits for them, and re-layouts: 3.68 us -> 0.01 us
    broadcast_in_dim x1, other arithmetic: 1.38 us -> 2.8 us  [shards(): return input_grad.astype(jnp.bfloat16)[None]]
    slice x1, local copies, waits for them, and re-layouts: 0.01 us -> 0.82 us  [shards(): input_grad = stats[1] * (norm_grad - stats[2] - normed * stats[3])]
where the time goes in v2:
time: 56.5 us; the launch traced here: 56.4 us
  Pallas kernels  52.7 us (93%)
  other arithmetic  2.8 us (5%)
  local copies, waits for them, and re-layouts  0.82 us (1%)
    pallas_call x1, Pallas kernels, shards(): pl.pallas_call(functools.partial(body, cells_per), out_shape=(jax.ShapeDt...  52.7 us
    broadcast_in_dim x1, other arithmetic, shards(): return input_grad.astype(jnp.bfloat16)[None]  2.8 us

profile of v2, /device:TPU:1, one launch (start us, length us, event | category | flops | bytes accessed | tf_op | source)
XLA Modules:
  0.0 56.4 jit_solution(18052371610106889368)
XLA Ops:
  0.0 0.0 copy-start
  0.0 52.7 %shard_map.55 = (f32[4,424,256]{2,1,0:T(8,128)}, f32[4,256]{1,0:T(4,128)}) custom-call(bf16[1,4,424,256]{3,2,1,0:T(8,128)(2,1)} %x_hbm.1, bf16[1,4,424,256]{3,2,1,0:T(8,128)(2,1)} %cot_hbm.1, bf16[3,3,768,256]{3,2,1,0:T(8,128)(2,1)} %bitcast.12, f32[1,256]{1,0:T(1,128)} %bitcast.17, f32[1,256]{1,0:T(1,128)} %bitcast.18), custom_call_target="tpu_custom_call" | custom-call | tf_op jit(solution)/shard_map/pallas_call | solution.py:401
  52.7 0.8 %fusion.6 = (f32[1,256]{1,0:T(1,128)S(1)}, f32[1,256]{1,0:T(1,128)S(1)}, f32[1,256]{1,0:T(1,128)S(1)}, f32[1,256]{1,0:T(1,128)S(1)}) fusion(f32[4,256]{1,0:T(4,128)} %get-tuple-element.7), kind=kLoop, calls=%fused_computation.7 | loop fusion | bytes 8192 | tf_op jit(solution)/shard_map/slice | solution.py:432
  53.6 0.0 copy-done
  53.6 2.8 %fusion.5 = bf16[1,4,424,256]{3,2,1,0:T(8,128)(2,1)} fusion(f32[4,424,256]{2,1,0:T(8,128)} %get-tuple-element.8, bf16[1,4,424,256]{3,2,1,0:T(8,128)(2,1)S(1)} %copy-done, f32[256]{0:T(256)S(1)} %bitcast.14, f32[256]{0:T(256)S(1)} %bitcast.15, f32[256]{0:T(256)S(1)} %bitcast.16, f32[256]{0:T(256)S(1)} %bitcast.13), kind=kLoop, calls=%fused_computation.6 | loop fusion | flops 3473408 | bytes 3477504 | tf_op jit(solution)/shard_map/broadcast_in_dim | solution.py:433
Async XLA Ops:
  0.0 53.6 %copy-start = (bf16[1,4,424,256]{3,2,1,0:T(8,128)(2,1)S(1)}, bf16[1,4,424,256]{3,2,1,0:T(8,128)(2,1)}, u32[]{:S(2)}) copy-start(bf16[1,4,424,256]{3,2,1,0:T(8,128)(2,1)} %x_hbm.1) | copy-start | bytes 2605060

commit v3 on v2

--- a/solution.py
+++ b/solution.py
@@ -40,8 +40,8 @@
 
 
 def body(
-    cells_per, x_hbm, cot_hbm, k_hbm, gain_hbm, bias_hbm, g_ref, stat_ref,
-    xin, gain_ref, bias_ref, staged, cot, weights, acc, slope, cur, near, far,
+    cells_per, x_hbm, cot_hbm, k_hbm, gain_hbm, bias_hbm, out_ref,
+    stat_ref, xin, gain_ref, bias_ref, staged, cot, weights, acc, slope, cur, near, far,
     lsem, ksem, own_send, frame_recv, relay_send, halo_send, halo_recv, ar_send, ar_recv,
 ):
     f, r = lax.axis_index("frames"), lax.axis_index("rows")
@@ -97,8 +97,7 @@
     def own_copy(p):
         slot = 2 - lax.rem(f, 2)
         return pltpu.make_async_remote_copy(
-            cot_hbm.at[0, row_of(p) - 1, :, pl.ds(pl.multiple_of(lax.rem(p, 2) * half, half), half)],
-            piece(slot, p), own_send.at[p], frame_recv.at[slot - 1, p],
+            piece(0, p), piece(slot, p), own_send.at[p], frame_recv.at[slot - 1, p],
             device_id=((f // 3) * 2, r), device_id_type=MESH,
         )
 
@@ -279,9 +278,9 @@
         def _():
             add_piece(row, h)
 
-        @pl.when((p == 4) | (p == 6))
-        def _():
-            e = (p - 4) // 2
+        @pl.when((p == 5) | (p == 7))
+        def _():
+            e = (p - 5) // 2
 
             def wait_slot(a, c):
                 await_halo(a, e)
@@ -301,7 +300,7 @@
 
                 lax.fori_loop(0, 2, halo_half, 0)
 
-        @pl.when(p == 1)
+        @pl.when(p == 0)
         def _():
             cur[1] = end_stage(0, near.at[0])
             send_stage(1, line_peers(f, r), far.at[0])
@@ -319,7 +318,7 @@
 
             lax.fori_loop(0, 2, own_halo, 0)
 
-        @pl.when(p == 4)
+        @pl.when(p == 3)
         def _():
             total = over_group(end_stage(1, far.at[0]), channels) / cells_per
             centre = total[0:1]
@@ -347,7 +346,7 @@
             + acc[y, pl.ds(PAD - 1, width), 2 * channels : 3 * channels]
         )
         norm_grad = act_grad * slope[y]
-        g_ref[y] = norm_grad
+        slope[y] = norm_grad
         normed = (xin[y].astype(jnp.float32) - stat_ref[0:1]) * stat_ref[1:2]
         return (
             carry[0] + jnp.sum(norm_grad, axis=0, keepdims=True),
@@ -389,6 +388,14 @@
     lax.fori_loop(0, slots, halo_sent, 0)
     total = over_group(end_stage(3, far.at[1]), channels) / cells_per
     stat_ref[2:4] = total
+
+    def out_row(y, c):
+        normed = (xin[y].astype(jnp.float32) - stat_ref[0:1]) * stat_ref[1:2]
+        input_grad = stat_ref[1:2] * (slope[y] - stat_ref[2:3] - normed * stat_ref[3:4])
+        out_ref[0, y] = input_grad.astype(jnp.bfloat16)
+        return c
+
+    lax.fori_loop(0, rows, out_row, 0)
     for k, slots_ref in enumerate((near.at[0], far.at[0], near.at[1], far.at[1])):
         whole_stage(k, slots_ref).wait_send()
 
@@ -398,15 +405,13 @@
     cells_per = FRAMES * STRIPS * rows * width * (channels // GROUPS)
     vmem, anywhere = pl.BlockSpec(memory_space=pltpu.VMEM), pl.BlockSpec(memory_space=pltpu.HBM)
     dma = pltpu.SemaphoreType.DMA
-    norm_grad, stats = pl.pallas_call(
+    return pl.pallas_call(
         functools.partial(body, cells_per),
-        out_shape=(
-            jax.ShapeDtypeStruct((rows, width, channels), jnp.float32),
-            jax.ShapeDtypeStruct((4, channels), jnp.float32),
-        ),
+        out_shape=jax.ShapeDtypeStruct(inputs.shape, jnp.bfloat16),
         in_specs=[anywhere] * 5,
-        out_specs=(vmem, vmem),
+        out_specs=vmem,
         scratch_shapes=[
+            pltpu.VMEM((4, channels), jnp.float32),
             pltpu.VMEM((rows, width, channels), jnp.bfloat16),
             pltpu.VMEM((1, channels), jnp.float32),
             pltpu.VMEM((1, channels), jnp.float32),
@@ -428,9 +433,6 @@
         inputs, cotangent, kernel.reshape(3, 3, 3 * channels, channels),
         norm_gain[None], norm_bias[None],
     )
-    normed = (inputs[0].astype(jnp.float32) - stats[0]) * stats[1]
-    input_grad = stats[1] * (norm_grad - stats[2] - normed * stats[3])
-    return input_grad.astype(jnp.bfloat16)[None]
 
 
 def solution(mesh):

time: 56.5 us -> 53.4 us (0.945)
  other arithmetic: 2.8 us -> 0 us
  Pallas kernels: 52.7 us -> 51.1 us
  local copies, waits for them, and re-layouts: 0.82 us -> 2.12 us
    broadcast_in_dim x1 -> x0, other arithmetic: 2.8 us -> none  [shards(): return input_grad.astype(jnp.bfloat16)[None]]
    unnamed x2 -> x1, local copies, waits for them, and re-layouts: 0.01 us -> 2.12 us
    pallas_call x1, Pallas kernels: 52.7 us -> 51.1 us  [shards(): pl.pallas_call(functools.partial(body, cells_per), out_shape=jax.ShapeDty...]
    slice x1 -> x0, local copies, waits for them, and re-layouts: 0.82 us -> none  [shards(): input_grad = stats[1] * (norm_grad - stats[2] - normed * stats[3])]
where the time goes in v3:
time: 53.4 us; the launch traced here: 53.3 us
  Pallas kernels  51.1 us (96%)
  local copies, waits for them, and re-layouts  2.12 us (4%)
    pallas_call x1, Pallas kernels, shards(): pl.pallas_call(functools.partial(body, cells_per), out_shape=jax.ShapeDty...  51.1 us
    unnamed x1, local copies, waits for them, and re-layouts  2.12 us

profile of v3, /device:TPU:1, one launch (start us, length us, event | category | flops | bytes accessed | tf_op | source)
XLA Modules:
  0.0 53.3 jit_solution(16171516716792691255)
XLA Ops:
  0.0 51.1 %shard_map.55 = bf16[1,4,424,256]{3,2,1,0:T(8,128)(2,1)} custom-call(bf16[1,4,424,256]{3,2,1,0:T(8,128)(2,1)} %x_hbm.1, bf16[1,4,424,256]{3,2,1,0:T(8,128)(2,1)} %cot_hbm.1, bf16[3,3,768,256]{3,2,1,0:T(8,128)(2,1)} %bitcast.3, f32[1,256]{1,0:T(1,128)} %bitcast.4, f32[1,256]{1,0:T(1,128)} %bitcast.5), custom_call_target="tpu_custom_call" | custom-call | tf_op jit(solution)/shard_map/pallas_call | solution.py:408
  51.2 2.1 %copy.7 = bf16[1,4,424,256]{3,2,1,0:T(8,128)(2,1)} copy(bf16[1,4,424,256]{3,2,1,0:T(8,128)(2,1)} %shard_map.55) | data formatting | bytes 1736704

commit v4 on v3

--- a/solution.py
+++ b/solution.py
@@ -12,20 +12,19 @@
 MESH = pl.DeviceIdType.MESH
 FRAMES, STRIPS = 4, 64
 PAD = 8
+FIRST = 1
+FAR_FIRST = (8, 7, 9, 6, 10, 5, 11, 4, 12, 3, 13, 2, 14, 1, 15)
 
 
 def plane_peers(f, r):
-    out = []
-    for dy in range(4):
-        for dx in range(4):
-            if dy or dx:
-                out.append((lax.rem(f + dy, 4), lax.rem(r + 16 * dx, 64)))
-    return out
+    offsets = [(dy, dx) for dy in (2, 1, 3, 0) for dx in (2, 1, 3, 0)]
+    offsets.sort(key=lambda o: -sum(min(d, 4 - d) for d in o))
+    return [(lax.rem(f + dy, 4), lax.rem(r + 16 * dx, 64)) for dy, dx in offsets[:-1]]
 
 
 def line_peers(f, r):
     base, low = 16 * (r // 16), lax.rem(r, 16)
-    return [(f, base + lax.rem(low + d, 16)) for d in range(1, 16)]
+    return [(f, base + lax.rem(low + d, 16)) for d in FAR_FIRST]
 
 
 def over_group(total, channels):
@@ -70,19 +69,6 @@
     for peer in greeted:
         pl.semaphore_signal(barrier, inc=1, device_id=peer, device_id_type=MESH)
 
-    load_x.wait()
-
-    def add_stats(y, carry):
-        values = xin[y].astype(jnp.float32)
-        return (
-            carry[0] + jnp.sum(values, axis=0, keepdims=True),
-            carry[1] + jnp.sum(values * values, axis=0, keepdims=True),
-        )
-
-    zero = jnp.zeros((1, channels), jnp.float32)
-    first, second = lax.fori_loop(0, rows, add_stats, (zero, zero))
-    cur[0] = jnp.concatenate([first, second], axis=0)
-
     def contract(left, right):
         return lax.dot_general(
             left, right, (((1,), (1,)), ((), ())), preferred_element_type=jnp.float32
@@ -199,7 +185,6 @@
 
     lax.fori_loop(0, rows, split_row, 0)
     pl.semaphore_wait(barrier, len(greeted))
-    send_stage(0, plane_peers(f, r), near.at[0])
 
     def send_own(p, carry):
         own_copy(p).start()
@@ -209,7 +194,26 @@
 
     @pl.when(f > 0)
     def _():
-        lax.fori_loop(0, ahead, send_own, 0)
+        lax.fori_loop(0, FIRST, send_own, 0)
+
+    load_x.wait()
+
+    def add_stats(y, carry):
+        values = xin[y].astype(jnp.float32)
+        return (
+            carry[0] + jnp.sum(values, axis=0, keepdims=True),
+            carry[1] + jnp.sum(values * values, axis=0, keepdims=True),
+        )
+
+    zero = jnp.zeros((1, channels), jnp.float32)
+    first, second = lax.fori_loop(0, rows, add_stats, (zero, zero))
+    cur[0] = jnp.concatenate([first, second], axis=0)
+
+    send_stage(0, plane_peers(f, r), near.at[0])
+
+    @pl.when(f > 0)
+    def _():
+        lax.fori_loop(FIRST, ahead, send_own, 0)
 
     @pl.when(r > 0)
     def _():

time: 53.4 us -> 53.1 us (level)
  no operation moved by 1% of the time
where the time goes in v4:
time: 53.1 us; the launch traced here: 53 us
  Pallas kernels  50.8 us (96%)
  local copies, waits for them, and re-layouts  2.12 us (4%)
    pallas_call x1, Pallas kernels, shards(): pl.pallas_call(functools.partial(body, cells_per), out_shape=jax.ShapeDty...  50.8 us
    unnamed x1, local copies, waits for them, and re-layouts  2.12 us

profile of v4, /device:TPU:1, one launch (start us, length us, event | category | flops | bytes accessed | tf_op | source)
XLA Modules:
  0.0 53.0 jit_solution(2808357777082437605)
XLA Ops:
  0.0 50.8 %shard_map.55 = bf16[1,4,424,256]{3,2,1,0:T(8,128)(2,1)} custom-call(bf16[1,4,424,256]{3,2,1,0:T(8,128)(2,1)} %x_hbm.1, bf16[1,4,424,256]{3,2,1,0:T(8,128)(2,1)} %cot_hbm.1, bf16[3,3,768,256]{3,2,1,0:T(8,128)(2,1)} %bitcast.3, f32[1,256]{1,0:T(1,128)} %bitcast.4, f32[1,256]{1,0:T(1,128)} %bitcast.5), custom_call_target="tpu_custom_call" | custom-call | tf_op jit(solution)/shard_map/pallas_call | solution.py:412
  50.8 2.1 %copy.7 = bf16[1,4,424,256]{3,2,1,0:T(8,128)(2,1)} copy(bf16[1,4,424,256]{3,2,1,0:T(8,128)(2,1)} %shard_map.55) | data formatting | bytes 1736704

commit v5 on v4

--- a/solution.py
+++ b/solution.py
@@ -56,8 +56,8 @@
     load_x = pltpu.make_async_copy(x_hbm.at[0], xin, lsem.at[2])
     load_gain = pltpu.make_async_copy(gain_hbm, gain_ref, lsem.at[3])
     load_bias = pltpu.make_async_copy(bias_hbm, bias_ref, lsem.at[4])
+    load_cot.start()
     load_x.start()
-    load_cot.start()
     for k in (2, 1, 0):
         load_weights(k).start()
     load_gain.start()
@@ -211,17 +211,17 @@
 
     send_stage(0, plane_peers(f, r), near.at[0])
 
+    @pl.when(r > 0)
+    def _():
+        halo_up(0).start()
+
+    @pl.when(r < STRIPS - 1)
+    def _():
+        halo_down(0).start()
+
     @pl.when(f > 0)
     def _():
         lax.fori_loop(FIRST, ahead, send_own, 0)
-
-    @pl.when(r > 0)
-    def _():
-        halo_up(0).start()
-
-    @pl.when(r < STRIPS - 1)
-    def _():
-        halo_down(0).start()
 
     edge_rows = jnp.zeros((rows, PAD, 3 * channels), jnp.float32)
     acc[:, 0:PAD, :] = edge_rows

time: 53.1 us -> 53.1 us (level)
  no operation moved by 1% of the time
where the time goes in v5:
time: 53.1 us; the launch traced here: 52.9 us
  Pallas kernels  50.8 us (96%)
  local copies, waits for them, and re-layouts  2.12 us (4%)
    pallas_call x1, Pallas kernels, shards(): pl.pallas_call(functools.partial(body, cells_per), out_shape=jax.ShapeDty...  50.8 us
    unnamed x1, local copies, waits for them, and re-layouts  2.12 us

profile of v5, /device:TPU:1, one launch (start us, length us, event | category | flops | bytes accessed | tf_op | source)
XLA Modules:
  0.0 52.9 jit_solution(7105539829669769781)
XLA Ops:
  0.0 50.8 %shard_map.55 = bf16[1,4,424,256]{3,2,1,0:T(8,128)(2,1)} custom-call(bf16[1,4,424,256]{3,2,1,0:T(8,128)(2,1)} %x_hbm.1, bf16[1,4,424,256]{3,2,1,0:T(8,128)(2,1)} %cot_hbm.1, bf16[3,3,768,256]{3,2,1,0:T(8,128)(2,1)} %bitcast.3, f32[1,256]{1,0:T(1,128)} %bitcast.4, f32[1,256]{1,0:T(1,128)} %bitcast.5), custom_call_target="tpu_custom_call" | custom-call | tf_op jit(solution)/shard_map/pallas_call | solution.py:412
  50.8 2.1 %copy.7 = bf16[1,4,424,256]{3,2,1,0:T(8,128)(2,1)} copy(bf16[1,4,424,256]{3,2,1,0:T(8,128)(2,1)} %shard_map.55) | data formatting | bytes 1736704
